TPU v7x, 32 devices: a whole 2x2x4 slice. The times are simulated.
32 devices in a mesh: items: 16 (over z, y, core), heads: 2 (over x).
Axes of the slice: x: 2, y: 2, z: 4, core: 2. Of those that a mesh axis runs over, the one named last changes fastest.
Arguments:
- hidden_in: bfloat16 [16384, 768], P('items'), may hold values from -6 to 6
- cluster_order: int32 [12, 16, 1024], P('heads', 'items'), may hold values from 0 to 1023, as said below
- qkv_weight: bfloat16 [3, 768, 768], P(None, None, 'heads'), may hold values from -0.21875 to 0.21875
- qv_bias: float32 [2, 768], P(None, 'heads'), may hold values from -3 to 3
- out_weight: bfloat16 [768, 768], P('heads'), may hold values from -0.875 to 0.875
- out_bias: float32 [768], replicated, may hold values from -2 to 2
- norm1_gain: float32 [768], replicated, may hold values from 0.5 to 1.5
- norm1_bias: float32 [768], replicated, may hold values from -2 to 2
- up_weight: bfloat16 [768, 3072], P(None, 'heads'), may hold values from -0.21875 to 0.21875
- up_bias: float32 [3072], P('heads'), may hold values from -2 to 2
- down_weight: bfloat16 [3072, 768], P('heads'), may hold values from -0.109375 to 0.109375
- down_bias: float32 [768], replicated, may hold values from -2 to 2
- norm2_gain: float32 [768], replicated, may hold values from 0.5 to 1.5
- norm2_bias: float32 [768], replicated, may hold values from -2 to 2
- cotangent: bfloat16 [16384, 768], P('items'), may hold values from -6 to 6
Outputs:
- mixed: bfloat16 [16384, 768], P('items')
- input_grad: bfloat16 [16384, 768], P('items')
- qkv_weight_grad: float32 [3, 768, 768], P(None, 'items', 'heads')
- qv_bias_grad: float32 [2, 768], P(None, 'heads')
- out_weight_grad: float32 [768, 768], P('heads', 'items')
- out_bias_grad: float32 [768], replicated
- norm1_gain_grad: float32 [768], replicated
- norm1_bias_grad: float32 [768], replicated
- up_weight_grad: float32 [768, 3072], P('items', 'heads')
- up_bias_grad: float32 [3072], P('heads')
- down_weight_grad: float32 [3072, 768], P('heads', 'items')
- down_bias_grad: float32 [768], replicated
- norm2_gain_grad: float32 [768], replicated
- norm2_bias_grad: float32 [768], replicated
Inputs may be any that keep to these rules, and one draw needn't show every extreme that they name: `cluster_order`: for each head and each device's block of 1024 tokens, an ordering of the block's positions 0 to 1023. A block holds one item of 1024 tokens or items of 512 tokens (the last one shorter where 512 does not divide 1024); an item's positions stand together in the ordering, in an order of their own for every head.
All inputs are finite; a program needn't handle non-finite values.
Results may differ from a plain program's by a relative error of at most 0.012.
Values sent between devices are 32-bit elements; how exact they have to be, the bound alone decides.
No kernel may reach another device: no remote copies, remote signals or barrier semaphores. Data moves between devices by JAX's collectives and lax.ppermute only.
A program may use at most 128 MiB of HBM per device.

v0:
```python
import jax
import jax.numpy as jnp
from jax import lax
from jax.sharding import PartitionSpec as P

HEAD_DIM = 64
CLUSTER = 128


EPSILON = 1e-05


def layer_norm(values, scale_vec, shift_vec):
    centred = values - jnp.mean(values, axis=-1, keepdims=True)
    spread = jnp.mean(centred * centred, axis=-1, keepdims=True)
    return centred * lax.rsqrt(spread + EPSILON) * scale_vec + shift_vec


def column_sum(values):
    return jnp.sum(values.astype(jnp.float32), axis=0)


def body(
    hidden_in,
    cluster_order,
    qkv_weight,
    qv_bias,
    out_weight,
    out_bias,
    norm1_gain,
    norm1_bias,
    up_weight,
    up_bias,
    down_weight,
    down_bias,
    norm2_gain,
    norm2_bias,
    cotangent,
):
    ordering = cluster_order[:, 0, :]
    local_heads = ordering.shape[0]
    token_rows = hidden_in.shape[0]
    clusters = token_rows // CLUSTER
    score_scale = HEAD_DIM ** (-0.5)
    positions = jnp.arange(token_rows, dtype=jnp.int32)
    selector = (ordering[:, :, None] == positions[None, None, :]).astype(jnp.bfloat16)

    def clustered(values):
        by_head = values.reshape(token_rows, local_heads, HEAD_DIM)
        moved_rows = jnp.einsum(
            "hit,thd->hid", selector, by_head, preferred_element_type=jnp.float32
        )
        return moved_rows.astype(jnp.bfloat16).reshape(local_heads, clusters, CLUSTER, HEAD_DIM)

    def restored(values):
        flat_rows = values.reshape(local_heads, token_rows, HEAD_DIM)
        back_rows = jnp.einsum(
            "hit,hid->thd", selector, flat_rows, preferred_element_type=jnp.float32
        )
        return back_rows.astype(jnp.bfloat16).reshape(token_rows, local_heads * HEAD_DIM)

    projected = jnp.einsum("td,cde->cte", hidden_in, qkv_weight, preferred_element_type=jnp.float32)
    query_c = clustered((projected[0] + qv_bias[0]).astype(jnp.bfloat16))
    key_c = clustered(projected[1].astype(jnp.bfloat16))
    value_c = clustered((projected[2] + qv_bias[1]).astype(jnp.bfloat16))
    scores = (
        jnp.einsum("hbqd,hbkd->hbqk", query_c, key_c, preferred_element_type=jnp.float32)
        * score_scale
    )
    row_peak = jnp.max(scores, axis=-1, keepdims=True)
    shifted = jnp.exp(scores - row_peak)
    totals = jnp.sum(shifted, axis=-1, keepdims=True)
    log_total = row_peak + jnp.log(totals)
    probs_b = (shifted / totals).astype(jnp.bfloat16)
    context_c = jnp.einsum("hbqk,hbkd->hbqd", probs_b, value_c, preferred_element_type=jnp.float32)
    context = restored(context_c.astype(jnp.bfloat16))
    inputs = hidden_in.astype(jnp.float32)
    attention_part = jnp.dot(context, out_weight, preferred_element_type=jnp.float32)
    attention = lax.psum(attention_part, "heads") + out_bias
    normed, norm1_pull = jax.vjp(layer_norm, inputs + attention, norm1_gain, norm1_bias)
    normed_b = normed.astype(jnp.bfloat16)
    hidden = jnp.dot(normed_b, up_weight, preferred_element_type=jnp.float32) + up_bias
    active, gelu_pull = jax.vjp(jax.nn.gelu, hidden)
    active_b = active.astype(jnp.bfloat16)
    feed_part = jnp.dot(active_b, down_weight, preferred_element_type=jnp.float32)
    feed_out = lax.psum(feed_part, "heads") + down_bias
    result, norm2_pull = jax.vjp(layer_norm, normed + feed_out, norm2_gain, norm2_bias)
    grad_sum, grad_gain2, grad_bias2 = norm2_pull(cotangent.astype(jnp.float32))
    grad_feed = grad_sum.astype(jnp.bfloat16)
    grad_down_bias = column_sum(grad_feed)
    grad_down = jnp.einsum("tf,td->fd", active_b, grad_feed, preferred_element_type=jnp.float32)
    grad_active = jnp.einsum(
        "td,fd->tf", grad_feed, down_weight, preferred_element_type=jnp.float32
    )
    grad_hidden = gelu_pull(grad_active)[0].astype(jnp.bfloat16)
    grad_up_bias = column_sum(grad_hidden)
    grad_up = jnp.einsum("td,tf->df", normed_b, grad_hidden, preferred_element_type=jnp.float32)
    back_part = jnp.einsum("tf,df->td", grad_hidden, up_weight, preferred_element_type=jnp.float32)
    grad_normed = grad_sum + lax.psum(back_part, "heads")
    grad_pre, grad_gain1, grad_bias1 = norm1_pull(grad_normed)
    grad_attention = grad_pre.astype(jnp.bfloat16)
    grad_out_bias = column_sum(grad_attention)
    grad_out = jnp.einsum("te,td->ed", context, grad_attention, preferred_element_type=jnp.float32)
    grad_context = jnp.einsum(
        "td,ed->te", grad_attention, out_weight, preferred_element_type=jnp.float32
    )
    grad_context_c = clustered(grad_context.astype(jnp.bfloat16))
    scores_again = (
        jnp.einsum("hbqd,hbkd->hbqk", query_c, key_c, preferred_element_type=jnp.float32)
        * score_scale
    )
    probs_again = jnp.exp(scores_again - log_total)
    again_b = probs_again.astype(jnp.bfloat16)
    grad_value_c = jnp.einsum(
        "hbqk,hbqd->hbkd", again_b, grad_context_c, preferred_element_type=jnp.float32
    )
    grad_probs = jnp.einsum(
        "hbqd,hbkd->hbqk", grad_context_c, value_c, preferred_element_type=jnp.float32
    )
    row_inner = jnp.sum(probs_again * grad_probs, axis=-1, keepdims=True)
    grad_scores = (probs_again * (grad_probs - row_inner)).astype(jnp.bfloat16)
    grad_query_c = (
        jnp.einsum("hbqk,hbkd->hbqd", grad_scores, key_c, preferred_element_type=jnp.float32)
        * score_scale
    )
    grad_key_c = (
        jnp.einsum("hbqk,hbqd->hbkd", grad_scores, query_c, preferred_element_type=jnp.float32)
        * score_scale
    )
    grad_qkv = jnp.stack(
        [
            restored(grad_query_c.astype(jnp.bfloat16)),
            restored(grad_key_c.astype(jnp.bfloat16)),
            restored(grad_value_c.astype(jnp.bfloat16)),
        ]
    )
    grad_qkv_weight = jnp.einsum(
        "td,cte->cde", hidden_in, grad_qkv, preferred_element_type=jnp.float32
    )
    grad_qv_bias = jnp.stack([column_sum(grad_qkv[0]), column_sum(grad_qkv[2])])
    input_part = jnp.einsum("cte,cde->td", grad_qkv, qkv_weight, preferred_element_type=jnp.float32)
    grad_inputs = grad_pre + lax.psum(input_part, "heads")
    summed_qkv, summed_out, summed_up, summed_down = (
        lax.psum_scatter(grad_qkv_weight, "items", scatter_dimension=1, tiled=True),
        lax.psum_scatter(grad_out, "items", scatter_dimension=1, tiled=True),
        lax.psum_scatter(grad_up, "items", scatter_dimension=0, tiled=True),
        lax.psum_scatter(grad_down, "items", scatter_dimension=1, tiled=True),
    )
    (
        small_qv,
        small_out,
        small_gain1,
        small_bias1,
        small_up,
        small_down,
        small_gain2,
        small_bias2,
    ) = lax.psum(
        (
            grad_qv_bias,
            grad_out_bias,
            grad_gain1,
            grad_bias1,
            grad_up_bias,
            grad_down_bias,
            grad_gain2,
            grad_bias2,
        ),
        "items",
    )
    return (
        result.astype(jnp.bfloat16),
        grad_inputs.astype(jnp.bfloat16),
        summed_qkv,
        small_qv,
        summed_out,
        small_out,
        small_gain1,
        small_bias1,
        summed_up,
        small_up,
        summed_down,
        small_down,
        small_gain2,
        small_bias2,
    )


def solution(mesh):
    return jax.shard_map(
        body,
        mesh=mesh,
        in_specs=(
            P("items", None),
            P("heads", "items", None),
            P(None, None, "heads"),
            P(None, "heads"),
            P("heads", None),
            P(),
            P(),
            P(),
            P(None, "heads"),
            P("heads"),
            P("heads", None),
            P(),
            P(),
            P(),
            P("items", None),
        ),
        out_specs=(
            P("items", None),
            P("items", None),
            P(None, "items", "heads"),
            P(None, "heads"),
            P("heads", "items"),
            P(),
            P(),
            P(),
            P("items", "heads"),
            P("heads"),
            P("heads", "items"),
            P(),
            P(),
            P(),
        ),
        check_vma=False,
    )
```

profile of v0, /device:TPU:0, one launch (start us, length us, event | category | flops | bytes accessed | tf_op | source)
XLA Modules:
  0.0 838.0 jit_solution(17607985827165720679)
XLA Ops:
  7.2 4.2 convolution_bitcast_fusion
  12.4 1.9 fusion.102
  14.5 6.6 fusion.52
  21.1 6.3 fusion.51
  27.5 6.3 fusion.53
  36.9 5.9 fusion.44
  43.8 2.7 fusion.103
  46.8 88.4 %all-reduce.8.cloned.1.call-done = f32[1024,768]{1,0:T(8,128)} async-done(((f32[1024,768]{1,0:T(8,128)}), f32[1024,768]{1,0:T(8,128)}) %all-reduce.8.cloned.1.call-update) | async-done | bytes 3145744 | tf_op jit(solution)/shard_map/psum | solution.py:79
  135.2 2.8 fusion.101
  138.8 6.0 multiply_convert_fusion
  144.8 1.6 copy-done.39
  146.4 4.3 fusion.104
  150.7 85.9 %all-reduce.10.cloned.1.call-done = f32[1024,768]{1,0:T(8,128)} async-done(((f32[1024,768]{1,0:T(8,128)}), f32[1024,768]{1,0:T(8,128)}) %all-reduce.10.cloned.1.call-update) | async-done | bytes 3145744 | tf_op jit(solution)/shard_map/psum | solution.py:86
  236.6 3.8 fusion.100
  241.9 1.3 fusion.26
  243.2 2.6 fusion.99
  245.8 1.6 copy-done.7
  248.8 6.8 convert_reduce_fusion
  255.6 1.6 copy-done.38
  257.2 4.3 fusion.105
  261.9 85.6 %all-reduce.12.cloned.1.call-done = f32[1024,768]{1,0:T(8,128)} async-done(((f32[1024,768]{1,0:T(8,128)}), f32[1024,768]{1,0:T(8,128)}) %all-reduce.12.cloned.1.call-update) | async-done | bytes 3145744 | tf_op jit(solution)/shard_map/psum | solution.py:99
  347.5 4.8 multiply_reduce_fusion
  352.3 1.5 fusion.98
  354.2 1.1 copy-done.25
  356.1 6.1 fusion.50
  362.2 1.2 fusion.54
  364.5 1.1 multiply_convert_fusion.1
  365.6 2.1 fusion.58
  367.7 1.5 fusion.57
  369.2 6.4 convert_reduce_fusion.4
  375.9 6.6 fusion.47
  382.5 7.2 convert_reduce_fusion.5
  389.7 1.6 copy.86
  391.3 2.4 copy.87
  393.7 5.0 convolution_bitcast_fusion.1
  398.6 6.2 copy.90
  405.0 1.1 copy-done.17
  406.0 5.4 convolution_bitcast_fusion.2
  412.5 3.5 fusion.106
  416.1 6.4 fusion.107
  422.5 8.0 fusion.93
  432.6 62.4 %all-reduce.1 = (f32[2,384]{1,0:T(2,128)}, f32[768]{0:T(1024)}, f32[768]{0:T(1024)}, f32[768]{0:T(1024)}, f32[1536]{0:T(1024)}, /*index=5*/f32[768]{0:T(1024)}, f32[768]{0:T(1024)}, f32[768]{0:T(1024)}) all-reduce(f32[2,384]{1,0:T(2,128)S(1)} %pad_maximum_fusion.3, ...), channel_id=1, replica_groups=mesh['items'=16,'heads'=2] {'items'}, use_global_device_ids=true, to_apply=%region_18.0 | all-reduce | flops 6912 | bytes 55296 | tf_op jit(solution)/shard_map/psum | solution.py:158
  495.0 27.3 %all-reduce.16.cloned.1.call-done = f32[3,768,384]{2,0,1:T(4,128)} async-done(((f32[3,768,384]{2,0,1:T(4,128)}), f32[3,768,384]{2,0,1:T(4,128)}) %all-reduce.16.cloned.1.call-update) | async-done | bytes 3538960
  524.0 86.0 %all-reduce.14.cloned.1.call-done = f32[1024,768]{1,0:T(8,128)} async-done(((f32[1024,768]{1,0:T(8,128)}), f32[1024,768]{1,0:T(8,128)}) %all-reduce.14.cloned.1.call-update) | async-done | bytes 3145744 | tf_op jit(solution)/shard_map/psum | solution.py:142
  610.0 4.3 add_convert_fusion
  614.3 57.8 %reduce-scatter.4.cloned.1.call-done = f32[384,48]{0,1:T(8,128)} async-done(((f32[384,768]{0,1:T(8,128)}), f32[384,48]{0,1:T(8,128)}) %reduce-scatter.4.cloned.1.call-update) | async-done | bytes 73744 | tf_op jit(solution)/shard_map/reduce_scatter | solution.py:145
  672.1 79.1 %reduce-scatter.8.cloned.1.call-done = f32[1536,48]{0,1:T(8,128)} async-done(((f32[1536,768]{0,1:T(8,128)}), f32[1536,48]{0,1:T(8,128)}) %reduce-scatter.8.cloned.1.call-update) | async-done | bytes 294928 | tf_op jit(solution)/shard_map/reduce_scatter | solution.py:147
  751.2 79.6 %reduce-scatter.6.cloned.1.call-done = f32[48,1536]{1,0:T(8,128)} async-done(((f32[768,1536]{1,0:T(8,128)}), f32[48,1536]{1,0:T(8,128)}) %reduce-scatter.6.cloned.1.call-update) | async-done | bytes 294928 | tf_op jit(solution)/shard_map/reduce_scatter | solution.py:146
  (126 shorter events, 16.3 us)
Async XLA Ops:
  7.2 131.4 %copy-start = (bf16[768,1536]{1,0:T(8,128)(2,1)S(1)}, bf16[768,1536]{1,0:T(8,128)(2,1)}, u32[]{:S(2)}) copy-start(bf16[768,1536]{1,0:T(8,128)(2,1)} %param.23) | copy-start | bytes 7077892
  7.2 128.0 %all-reduce.8.cloned.1.call-start = ((), (), s32[]{:S(2)}) async-start(), calls=%async_computation.3 | async-start | bytes 6291456 | tf_op jit(solution)/shard_map/psum | solution.py:79
  12.4 1.9 copy-start.33
  12.4 2.1 copy-start.27
  14.5 6.7 copy-start.16
  21.1 6.3 copy-start.15
  27.4 7.7 copy-start.22
  33.8 1.4 copy-start.9
  34.5 1.7 copy-start.4
  36.9 6.9 copy-start.24
  42.9 0.9 copy-start.20
  43.8 91.4 %copy-start.29 = (f32[768]{0:T(1024)S(1)}, f32[768]{0:T(1024)}, u32[]{:S(2)}) copy-start(f32[768]{0:T(1024)} %param.20) | copy-start | bytes 9220
  46.5 190.1 %all-reduce.10.cloned.1.call-start = ((), (), s32[]{:S(2)}) async-start(), calls=%async_computation.4 | async-start | bytes 6291456 | tf_op jit(solution)/shard_map/psum | solution.py:86
  138.0 6.8 copy-start.2
  138.0 0.8 copy-start.32
  138.0 0.8 copy-start.36
  138.8 7.6 copy-start.34
  144.8 1.6 copy-start.39
  150.7 86.0 %copy-start.30 = (f32[768]{0:T(1024)S(1)}, f32[768]{0:T(1024)}, u32[]{:S(2)}) copy-start(f32[768]{0:T(1024)} %param.26) | copy-start | bytes 9220
  150.7 196.8 %all-reduce.12.cloned.1.call-start = ((), (), s32[]{:S(2)}) async-start(), calls=%async_computation.5 | async-start | bytes 6291456 | tf_op jit(solution)/shard_map/psum | solution.py:99
  240.5 1.4 copy-start.8
  240.5 1.4 copy-start.28
  241.0 2.2 copy-start.31
  243.2 4.6 slice-start
  243.2 4.6 slice-start.1
  245.8 1.6 copy-start.7
  245.8 3.0 copy-start.35
  247.8 7.8 copy-start.12
  255.6 1.7 copy-start.38
  261.6 260.7 %all-reduce.16.cloned.1.call-start = ((), (), s32[]{:S(2)}) async-start(), calls=%async_computation.10 | async-start | bytes 9437184
  347.5 4.8 copy-start.3
  353.8 2.3 copy-start.6
  353.8 1.5 copy-start.25
  354.2 2.0 copy-start.14
  356.1 6.1 copy-start.5
  362.2 1.2 copy-start.23
  364.5 1.1 copy-start.10
  369.2 6.7 copy-start.19
  375.9 6.6 copy-start.18
  389.7 4.0 copy-start.11
  404.9 1.1 copy-start.17
  404.9 205.1 %all-reduce.14.cloned.1.call-start = ((), (), s32[]{:S(2)}) async-start(), calls=%async_computation.6 | async-start | bytes 6291456 | tf_op jit(solution)/shard_map/psum | solution.py:142
  411.4 1.1 copy-start.21
  411.4 4.7 copy-start.13
  411.4 260.7 %reduce-scatter.4.cloned.1.call-start = ((), (), s32[]{:S(2)}) async-start(), calls=%async_computation.7 | async-start | bytes 1253376 | tf_op jit(solution)/shard_map/reduce_scatter | solution.py:145
  416.0 335.1 %reduce-scatter.8.cloned.1.call-start = ((), (), s32[]{:S(2)}) async-start(), calls=%async_computation.9 | async-start | bytes 5013504 | tf_op jit(solution)/shard_map/reduce_scatter | solution.py:147
  422.5 408.3 %reduce-scatter.6.cloned.1.call-start = ((), (), s32[]{:S(2)}) async-start(), calls=%async_computation.8 | async-start | bytes 5013504 | tf_op jit(solution)/shard_map/reduce_scatter | solution.py:146
  523.3 307.4 %copy-start.1 = (bf16[768,1536]{1,0:T(8,128)(2,1)S(1)}, bf16[768,1536]{1,0:T(8,128)(2,1)}, u32[]{:S(2)}) copy-start(bf16[768,1536]{1,0:T(8,128)(2,1)} %param.23) | copy-start | bytes 7077892
  (2 other events, 1.4 us)
Sparse Core Ops, SparseCore 0:
  46.7 88.4 all-reduce.7
  150.8 85.7 all-reduce.9
  261.7 85.7 all-reduce.11
  405.0 117.2 all-reduce.15
  524.5 85.4 all-reduce.13
  614.0 57.9 reduce-scatter.3
  676.5 74.5 reduce-scatter.7
  756.1 74.5 reduce-scatter.5
where the time goes:
time: 846 us; the launch traced here: 838 us
  waiting for transfers between devices  590 us (70%)
  matrix products  116 us (14%)
  blocking collectives  62.4 us (7%)
  local copies, waits for them, and re-layouts  29 us (3%)
  other arithmetic  24.5 us (3%)
  between operations  15.9 us (2%)
    psum x1, waiting for transfers between devices, body(): attention = lax.psum(attention_part, 'heads') + out_bias  88.4 us
    psum x1, waiting for transfers between devices, body(): grad_inputs = grad_pre + lax.psum(input_part, 'heads')  86 us
    psum x1, waiting for transfers between devices, body(): feed_out = lax.psum(feed_part, 'heads') + down_bias  85.9 us
    psum x1, waiting for transfers between devices, body(): grad_normed = grad_sum + lax.psum(back_part, 'heads')  85.6 us
    reduce_scatter x1, waiting for transfers between devices, body(): lax.psum_scatter(grad_up, 'items', scatter_dimension=0, tiled=True)  79.6 us
    reduce_scatter x1, waiting for transfers between devices, body(): lax.psum_scatter(grad_down, 'items', scatter_dimension=1, tiled=True)  79.1 us
    psum x1, blocking collectives, body(): lax.psum((grad_qv_bias, grad_out_bias, grad_gain1, grad_bias1, grad_up_bi...  62.4 us
    reduce_scatter x1, waiting for transfers between devices, body(): lax.psum_scatter(grad_out, 'items', scatter_dimension=1, tiled=True)  57.8 us
  transfers between devices with their start and end apart: 8, of which 8 were waited for; matrix products, arithmetic and copies ran while one was open for 4% of the time, Pallas kernels for 0%

commit v1 on v0

v1 whole, which is shorter than its diff:
```python
import jax
import jax.numpy as jnp
from jax import lax
from jax.experimental import pallas as pl
from jax.experimental.pallas import tpu as pltpu
from jax.sharding import PartitionSpec as P

HEAD_DIM = 64
CLUSTER = 128
SCALE = HEAD_DIM**-0.5
EPSILON = 1e-05
VMEM_LIMIT = 60 * 1024 * 1024
BF16 = jnp.bfloat16
F32 = jnp.float32


def dot(left, right):
    return jnp.dot(left, right, preferred_element_type=F32)


def dot_nt(left, right):
    return lax.dot_general(left, right, (((1,), (1,)), ((), ())), preferred_element_type=F32)


def dot_tn(left, right):
    return lax.dot_general(left, right, (((0,), (0,)), ((), ())), preferred_element_type=F32)


def params_of(**more):
    return pltpu.CompilerParams(vmem_limit_bytes=VMEM_LIMIT, **more)


def cost(flops, bytes_accessed):
    return pl.CostEstimate(flops=int(flops), bytes_accessed=int(bytes_accessed), transcendentals=0)


def shape(dims, dtype):
    return jax.ShapeDtypeStruct(dims, dtype)


def whole(*dims):
    return pl.BlockSpec(dims, lambda *_: (0,) * len(dims), pipeline_mode=pl.Buffered(1))


def swapped(values):
    return lax.ppermute(values, "heads", [(0, 1), (1, 0)])


def traded(values, step, n_items):
    return lax.ppermute(values, "items", [(i, i ^ step) for i in range(n_items)])


def all_sum(values, n_items):
    step = 1
    while step < n_items:
        values = values + traded(values, step, n_items)
        step *= 2
    return values


def scattered(values, n_items, axis, order):
    item = lax.axis_index("items")
    dims = values.shape
    bits = list(range(n_items.bit_length() - 1))
    rows = dims[axis] // n_items
    values = values.reshape(dims[:axis] + (2,) * len(bits) + (rows,) + dims[axis + 1 :])
    left = bits[::-1]
    for bit in order(bits):
        place = axis + left.index(bit)
        mine = (item >> bit) & 1
        send = lax.dynamic_index_in_dim(values, 1 - mine, place, keepdims=False)
        keep = lax.dynamic_index_in_dim(values, mine, place, keepdims=False)
        values = keep + traded(send, 1 << bit, n_items)
        left.remove(bit)
    return values


def picked(columns, lanes):
    return jnp.where(columns == lanes, 1.0, 0.0).astype(BF16)


def attend_kernel(
    x_ref, w_ref, bias_ref, row_ref, col_ref, ctx_ref, sent_ref, moved_ref, probs_ref, sel_ref, cen_ref
):
    rows = x_ref.shape[0]
    step = 256
    halves = []
    for h in range(2):
        cut = slice(h * HEAD_DIM, (h + 1) * HEAD_DIM)
        weight = jnp.concatenate([w_ref[c][:, cut] for c in range(3)], axis=1)
        bias = jnp.concatenate(
            [bias_ref[0:1, cut], jnp.zeros((1, HEAD_DIM), F32), bias_ref[1:2, cut]], axis=1
        )
        lanes = lax.broadcasted_iota(jnp.int32, (step, rows), 1)
        for r in range(0, rows, step):
            sel_ref[r : r + step, :] = picked(col_ref[0, r : r + step, h : h + 1], lanes)
        qkv = (dot(x_ref[...], weight) + bias).astype(BF16)
        moved_ref[h] = dot(sel_ref[...], qkv).astype(BF16)
        for c in range(rows // CLUSTER):
            span = slice(c * CLUSTER, (c + 1) * CLUSTER)
            query = moved_ref[h, span, :HEAD_DIM]
            key = moved_ref[h, span, HEAD_DIM : 2 * HEAD_DIM]
            value = moved_ref[h, span, 2 * HEAD_DIM :]
            scores = dot_nt(query, key) * SCALE
            shifted = jnp.exp(scores - jnp.max(scores, axis=-1, keepdims=True))
            probs = shifted / jnp.sum(shifted, axis=-1, keepdims=True)
            probs_ref[h, c] = probs
            cen_ref[span, :] = dot(probs.astype(BF16), value).astype(BF16)
        for r in range(0, rows, step):
            subs = lax.broadcasted_iota(jnp.int32, (step, rows), 0) + r
            sel_ref[r : r + step, :] = picked(row_ref[0, h : h + 1, :], subs)
        halves.append(dot(sel_ref[...], cen_ref[...]))
    context = jnp.concatenate(halves, axis=1).astype(BF16)
    ctx_ref[...] = context
    sent_ref[...] = context.astype(F32)


def attend(x, weight, bias, order_rows, order_cols):
    rows, width = x.shape
    pairs = order_rows.shape[0]
    local = weight.shape[2]
    clusters = rows // CLUSTER
    return pl.pallas_call(
        attend_kernel,
        grid=(pairs,),
        in_specs=[
            whole(rows, width),
            pl.BlockSpec((3, width, 128), lambda p: (0, 0, p)),
            pl.BlockSpec((2, 128), lambda p: (0, p)),
            pl.BlockSpec((1, 2, rows), lambda p: (p, 0, 0)),
            pl.BlockSpec((1, rows, 2), lambda p: (p, 0, 0)),
        ],
        out_specs=[
            pl.BlockSpec((rows, 128), lambda p: (0, p)),
            pl.BlockSpec((rows, 128), lambda p: (0, p)),
            pl.BlockSpec((2, rows, 3 * HEAD_DIM), lambda p: (p, 0, 0)),
            pl.BlockSpec((2, clusters, CLUSTER, CLUSTER), lambda p: (p, 0, 0, 0)),
        ],
        out_shape=[
            shape((rows, local), BF16),
            shape((rows, local), F32),
            shape((2 * pairs, rows, 3 * HEAD_DIM), BF16),
            shape((2 * pairs, clusters, CLUSTER, CLUSTER), F32),
        ],
        scratch_shapes=[pltpu.VMEM((rows, rows), BF16), pltpu.VMEM((rows, HEAD_DIM), BF16)],
        compiler_params=params_of(),
        cost_estimate=cost(12e9, 12e6),
        name="attend",
    )(x, weight, bias, order_rows, order_cols)


def attend_back_kernel(
    xt_ref, da_ref, ow_ref, ctx_ref, w_ref, row_ref, col_ref, moved_ref, probs_ref,
    part_ref, grad_ref, bias_ref, sel_ref, cen_ref,
):
    rows = da_ref.shape[0]
    step = 256
    d_attn = da_ref[...]
    d_context = dot_nt(d_attn, ow_ref[...]).astype(BF16)
    grad_ref[3] = dot(ctx_ref[...].T, d_attn).T
    found = []
    for h in range(2):
        lanes = lax.broadcasted_iota(jnp.int32, (step, rows), 1)
        for r in range(0, rows, step):
            sel_ref[r : r + step, :] = picked(col_ref[0, r : r + step, h : h + 1], lanes)
        d_moved = dot(sel_ref[...], d_context[:, h * HEAD_DIM : (h + 1) * HEAD_DIM]).astype(BF16)
        for c in range(rows // CLUSTER):
            span = slice(c * CLUSTER, (c + 1) * CLUSTER)
            query = moved_ref[h, span, :HEAD_DIM]
            key = moved_ref[h, span, HEAD_DIM : 2 * HEAD_DIM]
            value = moved_ref[h, span, 2 * HEAD_DIM :]
            probs = probs_ref[h, c]
            above = d_moved[span, :]
            d_value = dot_tn(probs.astype(BF16), above)
            d_probs = dot_nt(above, value)
            inner = jnp.sum(probs * d_probs, axis=-1, keepdims=True)
            d_scores = (probs * (d_probs - inner)).astype(BF16)
            d_query = dot(d_scores, key) * SCALE
            d_key = dot_tn(d_scores, query) * SCALE
            cen_ref[span, :] = jnp.concatenate([d_query, d_key, d_value], axis=1).astype(BF16)
        for r in range(0, rows, step):
            subs = lax.broadcasted_iota(jnp.int32, (step, rows), 0) + r
            sel_ref[r : r + step, :] = picked(row_ref[0, h : h + 1, :], subs)
        found.append(dot(sel_ref[...], cen_ref[...]))
    d_qkv = jnp.concatenate(
        [f[:, c * HEAD_DIM : (c + 1) * HEAD_DIM] for c in range(3) for f in found], axis=1
    ).astype(BF16)
    sums = jnp.sum(d_qkv.astype(F32), axis=0, keepdims=True)
    bias_ref[0:1, :] = sums[:, :128]
    bias_ref[1:2, :] = sums[:, 256:]
    grads = dot(xt_ref[...], d_qkv)
    for c in range(3):
        grad_ref[c] = grads[:, c * 128 : (c + 1) * 128]
    part = dot_nt(d_qkv, jnp.concatenate([w_ref[c] for c in range(3)], axis=1))

    @pl.when(pl.program_id(0) == 0)
    def _():
        part_ref[...] = part

    @pl.when(pl.program_id(0) > 0)
    def _():
        part_ref[...] += part


def attend_back(xt, d_attn, out_weight, context, weight, order_rows, order_cols, moved, probs):
    width, rows = xt.shape
    pairs = order_rows.shape[0]
    local = weight.shape[2]
    clusters = rows // CLUSTER
    return pl.pallas_call(
        attend_back_kernel,
        grid=(pairs,),
        in_specs=[
            whole(width, rows),
            whole(rows, width),
            pl.BlockSpec((128, width), lambda p: (p, 0)),
            pl.BlockSpec((rows, 128), lambda p: (0, p)),
            pl.BlockSpec((3, width, 128), lambda p: (0, 0, p)),
            pl.BlockSpec((1, 2, rows), lambda p: (p, 0, 0)),
            pl.BlockSpec((1, rows, 2), lambda p: (p, 0, 0)),
            pl.BlockSpec((2, rows, 3 * HEAD_DIM), lambda p: (p, 0, 0)),
            pl.BlockSpec((2, clusters, CLUSTER, CLUSTER), lambda p: (p, 0, 0, 0)),
        ],
        out_specs=[
            pl.BlockSpec((rows, width), lambda p: (0, 0)),
            pl.BlockSpec((4, width, 128), lambda p: (0, 0, p)),
            pl.BlockSpec((2, 128), lambda p: (0, p)),
        ],
        out_shape=[
            shape((rows, width), F32),
            shape((4, width, local), F32),
            shape((2, local), F32),
        ],
        scratch_shapes=[pltpu.VMEM((rows, rows), BF16), pltpu.VMEM((rows, 3 * HEAD_DIM), BF16)],
        compiler_params=params_of(),
        cost_estimate=cost(20e9, 20e6),
        name="attend_back",
    )(xt, d_attn, out_weight, context, weight, order_rows, order_cols, moved, probs)


def gelu_both(hidden):
    scale = 0.7978845608028654
    square = hidden * hidden
    bent = jnp.tanh(hidden * (scale + (scale * 0.044715) * square))
    half = 0.5 + 0.5 * bent
    active = hidden * half
    slope = half + 0.5 * hidden * (1.0 - bent * bent) * (scale + (3 * scale * 0.044715) * square)
    return active.astype(BF16), slope.astype(BF16)


def normalized(values):
    centred = values - jnp.mean(values, axis=-1, keepdims=True)
    factor = lax.rsqrt(jnp.mean(centred * centred, axis=-1, keepdims=True) + EPSILON)
    return centred * factor, factor


def norm_back(grad, unit, factor):
    mean = jnp.mean(grad, axis=-1, keepdims=True)
    inner = jnp.mean(grad * unit, axis=-1, keepdims=True)
    return factor * (grad - mean - unit * inner)


def lead_kernel(
    x_ref, ctx_ref, far_ctx_ref, out_ref, far_out_ref, vec_ref, up_ref, up_bias_ref, down_ref,
    unit_ref, factor_ref, nb_ref, act_ref, slope_ref, feed_ref,
):
    attention = dot(ctx_ref[...], out_ref[...])
    attention += dot(far_ctx_ref[...].astype(BF16), far_out_ref[...].astype(BF16))
    unit, factor = normalized(x_ref[...].astype(F32) + attention + vec_ref[0:1, :])
    unit_ref[...] = unit
    factor_ref[...] = factor
    nb = (unit * vec_ref[1:2, :] + vec_ref[2:3, :]).astype(BF16)
    nb_ref[...] = nb
    active, slope = gelu_both(dot(nb, up_ref[...]) + up_bias_ref[...])
    act_ref[...] = active
    slope_ref[...] = slope
    feed_ref[...] = dot(active, down_ref[...])


def lead(x, context, far_context, out_weight, far_small, vectors, up, up_bias, down):
    rows, width = x.shape
    local, units = out_weight.shape[0], up.shape[1]
    tile = 256
    across = lambda cols: pl.BlockSpec((tile, cols), lambda i: (i, 0))
    return pl.pallas_call(
        lead_kernel,
        grid=(rows // tile,),
        in_specs=[
            across(width), across(local), across(local), whole(local, width), whole(local, width),
            whole(8, width), whole(width, units), whole(1, units), whole(units, width),
        ],
        out_specs=[
            across(width), across(1), across(width), across(units), across(units), across(width),
        ],
        out_shape=[
            shape((rows, width), F32), shape((rows, 1), F32), shape((rows, width), BF16),
            shape((rows, units), BF16), shape((rows, units), BF16), shape((rows, width), F32),
        ],
        compiler_params=params_of(),
        cost_estimate=cost(6e9, 20e6),
        name="lead",
    )(x, context, far_context, out_weight, far_small, vectors, up, up_bias, down)


def middle_kernel(
    unit_ref, factor_ref, feed_ref, slope_ref, cot_ref, vec_ref, far_ref, far_bias_ref, up_ref, down_ref,
    mixed_ref, d_feed_ref, d_hidden_ref, d_pre_ref, d_attn_ref, sums_ref, up_sums_ref, up_s, down_s,
):
    width, units = up_ref.shape
    first = pl.program_id(0) == 0

    @pl.when(first)
    def _():
        for i in range(units // width):
            up_s[:, i * width : (i + 1) * width] = far_ref[i * width : (i + 1) * width].astype(BF16)
        down_s[...] = far_ref[units:, :].astype(BF16)
        sums_ref[...] = jnp.zeros_like(sums_ref)
        up_sums_ref[...] = jnp.zeros_like(up_sums_ref)

    unit1 = unit_ref[...]
    normed = unit1 * vec_ref[1:2, :] + vec_ref[2:3, :]
    nb = normed.astype(BF16)
    far_bias = jnp.concatenate(
        [far_bias_ref[i : i + 1, :] for i in range(units // width)], axis=1
    )
    far_active, far_slope = gelu_both(dot(nb, up_s[...]) + far_bias)
    feed = feed_ref[...] + dot(far_active, down_s[...]) + vec_ref[3:4, :]
    unit2, factor2 = normalized(normed + feed)
    mixed_ref[...] = (unit2 * vec_ref[4:5, :] + vec_ref[5:6, :]).astype(BF16)
    grad = cot_ref[...].astype(F32)
    sums_ref[0:1, :] += jnp.sum(grad * unit2, axis=0, keepdims=True)
    sums_ref[1:2, :] += jnp.sum(grad, axis=0, keepdims=True)
    d_sum = norm_back(grad * vec_ref[4:5, :], unit2, factor2)
    d_feed = d_sum.astype(BF16)
    d_feed_ref[...] = d_feed
    sums_ref[2:3, :] += jnp.sum(d_feed.astype(F32), axis=0, keepdims=True)
    d_hidden = (dot_nt(d_feed, down_ref[...]) * slope_ref[...].astype(F32)).astype(BF16)
    d_hidden_ref[...] = d_hidden
    up_sums_ref[...] += jnp.sum(d_hidden.astype(F32), axis=0, keepdims=True)
    far_d_hidden = (dot_nt(d_feed, down_s[...]) * far_slope.astype(F32)).astype(BF16)
    d_normed = d_sum + dot_nt(d_hidden, up_ref[...]) + dot_nt(far_d_hidden, up_s[...])
    sums_ref[3:4, :] += jnp.sum(d_normed * unit1, axis=0, keepdims=True)
    sums_ref[4:5, :] += jnp.sum(d_normed, axis=0, keepdims=True)
    d_pre = norm_back(d_normed * vec_ref[1:2, :], unit1, factor_ref[...])
    d_pre_ref[...] = d_pre
    d_attn = d_pre.astype(BF16)
    d_attn_ref[...] = d_attn
    sums_ref[5:6, :] += jnp.sum(d_attn.astype(F32), axis=0, keepdims=True)


def middle(unit, factor, feed, slope, cotangent, vectors, far, far_small, up, down):
    rows, width = unit.shape
    units = up.shape[1]
    tile = 256
    across = lambda cols: pl.BlockSpec((tile, cols), lambda i: (i, 0))
    return pl.pallas_call(
        middle_kernel,
        grid=(rows // tile,),
        in_specs=[
            across(width), across(1), across(width), across(units), across(width), whole(8, width),
            whole(2 * units, width),
            pl.BlockSpec((8, width), lambda i: (far_small.shape[0] // 8 - 1, 0)),
            whole(width, units), whole(units, width),
        ],
        out_specs=[
            across(width), across(width), across(units), across(width), across(width),
            pl.BlockSpec((8, width), lambda i: (0, 0)), pl.BlockSpec((1, units), lambda i: (0, 0)),
        ],
        out_shape=[
            shape((rows, width), BF16), shape((rows, width), BF16), shape((rows, units), BF16),
            shape((rows, width), F32), shape((rows, width), BF16),
            shape((8, width), F32), shape((1, units), F32),
        ],
        scratch_shapes=[pltpu.VMEM((width, units), BF16), pltpu.VMEM((units, width), BF16)],
        compiler_params=params_of(),
        cost_estimate=cost(15e9, 30e6),
        name="middle",
    )(unit, factor, feed, slope, cotangent, vectors, far, far_small, up, down)


def feed_grads_kernel(nb_ref, d_feed_ref, act_ref, d_hidden_ref, up_ref, down_ref, nbt_s, d_feedt_s):
    @pl.when(pl.program_id(0) == 0)
    def _():
        nbt_s[...] = nb_ref[...].T
        d_feedt_s[...] = d_feed_ref[...].T

    down_ref[...] = dot(d_feedt_s[...], act_ref[...])
    up_ref[...] = dot(nbt_s[...], d_hidden_ref[...])


def feed_grads(nb, d_feed, active, d_hidden):
    rows, width = nb.shape
    units = active.shape[1]
    tile = 256
    along = lambda height: pl.BlockSpec((height, tile), lambda j: (0, j))
    return pl.pallas_call(
        feed_grads_kernel,
        grid=(units // tile,),
        in_specs=[whole(rows, width), whole(rows, width), along(rows), along(rows)],
        out_specs=[along(width), along(width)],
        out_shape=[shape((width, units), F32), shape((width, units), F32)],
        scratch_shapes=[pltpu.VMEM((width, rows), BF16), pltpu.VMEM((width, rows), BF16)],
        compiler_params=params_of(),
        cost_estimate=cost(5e9, 20e6),
        name="feed_grads",
    )(nb, d_feed, active, d_hidden)


def make_body(n_items):
    def body(
        hidden_in,
        cluster_order,
        qkv_weight,
        qv_bias,
        out_weight,
        out_bias,
        norm1_gain,
        norm1_bias,
        up_weight,
        up_bias,
        down_weight,
        down_bias,
        norm2_gain,
        norm2_bias,
        cotangent,
    ):
        rows, width = hidden_in.shape
        units = up_weight.shape[1]
        local = out_weight.shape[0]
        item = lax.axis_index("items")

        stacked = jnp.concatenate(
            [up_weight[:, i : i + width] for i in range(0, units, width)] + [down_weight], axis=0
        )
        piece_rows = stacked.shape[0] // n_items
        piece = lax.dynamic_slice_in_dim(stacked, item * piece_rows, piece_rows, 0)
        far = lax.all_gather(swapped(piece.astype(F32)), "items", axis=0, tiled=True)
        bias_rows = jnp.zeros((8 * width,), F32).at[:units].set(up_bias).reshape(8, width)
        far_small = swapped(jnp.concatenate([out_weight.astype(F32), bias_rows], axis=0))
        zero = jnp.zeros_like(out_bias)
        vectors = jnp.stack(
            [out_bias, norm1_gain, norm1_bias, down_bias, norm2_gain, norm2_bias, zero, zero]
        )

        ordering = cluster_order[:, 0, :]
        order_rows = ordering.reshape(-1, 2, rows)
        order_cols = jnp.transpose(order_rows, (0, 2, 1))
        context, sent, moved, probs = attend(
            hidden_in, qkv_weight, qv_bias, order_rows, order_cols
        )
        far_context = swapped(sent)
        unit, factor, nb, active, slope, feed = lead(
            hidden_in, context, far_context, out_weight, far_small, vectors, up_weight,
            up_bias.reshape(1, units), down_weight,
        )
        mixed, d_feed, d_hidden, d_pre, d_attn, sums, up_sums = middle(
            unit, factor, feed, slope, cotangent, vectors, far, far_small, up_weight, down_weight
        )
        grad_up, grad_down = feed_grads(nb, d_feed, active, d_hidden)
        in_order = lambda bits: bits
        turned = lambda bits: bits[:1] + bits[2:] + bits[1:2]
        summed_down = scattered(grad_down, n_items, 0, in_order)
        summed_up = scattered(grad_up, n_items, 0, turned)
        part, grad_rest, grad_qv = attend_back(
            hidden_in.T, d_attn, out_weight, context, qkv_weight, order_rows, order_cols, moved, probs
        )
        grad_inputs = d_pre + part + swapped(part)
        summed_rest = scattered(grad_rest, n_items, 1, in_order)

        parts = [sums.reshape(-1), up_sums.reshape(-1), grad_qv.reshape(-1)]
        sizes = [piece_of.shape[0] for piece_of in parts]
        total = sum(sizes)
        padded = -(-total // 1024) * 1024
        packed = jnp.concatenate(parts + [jnp.zeros((padded - total,), F32)])
        packed = all_sum(packed.reshape(8, padded // 8), n_items).reshape(-1)
        small = packed[: 8 * width].reshape(8, width)
        up_small = packed[sizes[0] : sizes[0] + units]
        qv_small = packed[sizes[0] + units : total].reshape(2, local)
        return (
            mixed,
            grad_inputs.astype(BF16),
            summed_rest[:3],
            qv_small,
            summed_rest[3].T,
            small[5],
            small[3],
            small[4],
            summed_up,
            up_small,
            summed_down.T,
            small[2],
            small[0],
            small[1],
        )

    return body


def solution(mesh):
    return jax.shard_map(
        make_body(mesh.shape["items"]),
        mesh=mesh,
        in_specs=(
            P("items", None),
            P("heads", "items", None),
            P(None, None, "heads"),
            P(None, "heads"),
            P("heads", None),
            P(),
            P(),
            P(),
            P(None, "heads"),
            P("heads"),
            P("heads", None),
            P(),
            P(),
            P(),
            P("items", None),
        ),
        out_specs=(
            P("items", None),
            P("items", None),
            P(None, "items", "heads"),
            P(None, "heads"),
            P("heads", "items"),
            P(),
            P(),
            P(),
            P("items", "heads"),
            P("heads"),
            P("heads", "items"),
            P(),
            P(),
            P(),
        ),
        check_vma=False,
    )
```

time: 846 us -> 371 us (0.44)
  waiting for transfers between devices: 590 us -> 161 us
  Pallas kernels: 0 us -> 126 us
  matrix products: 116 us -> 0 us
  blocking collectives: 62.4 us -> 0 us
  starting transfers between devices: 0.72 us -> 29.8 us
  other arithmetic: 24.5 us -> 14.5 us
    psum x4 -> x0, waiting for transfers between devices: 346 us -> none  [the longest x1 88.4 us: body(): attention = lax.psum(attention_part, 'heads') + out_bias]
    reduce_scatter x3 -> x0, waiting for transfers between devices: 216 us -> none  [the longest x1 79.6 us: body(): lax.psum_scatter(grad_up, 'items', scatter_dimension=0, tiled=True)]
    ppermute x0 -> x20, waiting for transfers between devices: none -> 161 us  [the longest x4 101 us: swapped(): return lax.ppermute(values, 'heads', [(0, 1), (1, 0)])]
    pallas_call x0 -> x5, Pallas kernels: none -> 126 us  [the longest x1 39.5 us: attend_back(): pl.pallas_call(attend_back_kernel, grid=(pairs,), in_specs=[whole(width,...]
    dot_general x26 -> x0, matrix products: 116 us -> none  [the longest x4 26 us: restored(): jnp.einsum('hit,hid->thd', selector, flat_rows, preferred_element_type=jn...]
    psum x1 -> x0, blocking collectives: 62.4 us -> none  [body(): lax.psum((grad_qv_bias, grad_out_bias, grad_gain1, grad_bias1, grad_up_bi...]
    ppermute x0 -> x20, starting transfers between devices: none -> 29.8 us  [the longest x16 23.2 us: traded(): lax.ppermute(values, 'items', [(i, i ^ step) for i in range(n_items)])]
    unnamed x9 -> x1, waiting for transfers between devices: 27.4 us -> 0.02 us
  transfers between devices with their start and end apart: 8 -> 21, of which waited for: 8 -> 12; matrix products, arithmetic and copies ran while one was open for 4% -> 8% of each run, Pallas kernels for 0% -> 23%
where the time goes in v1:
time: 371 us
  waiting for transfers between devices  161 us (43%)
  Pallas kernels  126 us (34%)
  starting transfers between devices  29.8 us (8%)
  local copies, waits for them, and re-layouts  25.3 us (7%)
  other arithmetic  14.5 us (4%)
  between operations  14.5 us (4%)
    ppermute x4, waiting for transfers between devices, swapped(): return lax.ppermute(values, 'heads', [(0, 1), (1, 0)])  101 us
    ppermute x16, waiting for transfers between devices, traded(): lax.ppermute(values, 'items', [(i, i ^ step) for i in range(n_items)])  59.2 us
    pallas_call x1, Pallas kernels, attend_back(): pl.pallas_call(attend_back_kernel, grid=(pairs,), in_specs=[whole(width,...  39.5 us
    pallas_call x1, Pallas kernels, middle(): pl.pallas_call(middle_kernel, grid=(rows // tile,), in_specs=[across(widt...  29.6 us
    pallas_call x1, Pallas kernels, attend(): pl.pallas_call(attend_kernel, grid=(pairs,), in_specs=[whole(rows, width)...  29.5 us
    ppermute x16, starting transfers between devices, traded(): lax.ppermute(values, 'items', [(i, i ^ step) for i in range(n_items)])  23.2 us
    pallas_call x1, Pallas kernels, lead(): pl.pallas_call(lead_kernel, grid=(rows // tile,), in_specs=[across(width)...  15.3 us
    pallas_call x1, Pallas kernels, feed_grads(): pl.pallas_call(feed_grads_kernel, grid=(units // tile,), in_specs=[whole(...  12.1 us
  transfers between devices with their start and end apart: 21, of which 12 were waited for; matrix products, arithmetic and copies ran while one was open for 8% of the time, Pallas kernels for 23%

profile of v1, /device:TPU:0, one launch (start us, length us, event | category | flops | bytes accessed | tf_op | source)
XLA Modules:
  0.0 370.7 jit_solution(14586894089843740664)
XLA Ops:
  7.2 1.8 fusion.4
  9.4 3.0 collective-permute-start.2
  12.4 13.3 %collective-permute-done.2 = f32[192,768]{1,0:T(8,128)S(1)} collective-permute-done((f32[192,768]{1,0:T(8,128)S(1)}, f32[192,768]{1,0:T(8,128)S(1)}, u32[]{:S(2)}, u32[]{:S(2)}) %collective-permute-start.2) | collective-permute-done | bytes 589856 | tf_op jit(solution)/shard_map/ppermute | solution.py:46
  25.7 0.9 copy-done.6
  26.7 1.7 copy.32
  28.4 29.5 %attend.1 = (bf16[1024,384]{1,0:T(8,128)(2,1)}, f32[1024,384]{1,0:T(8,128)}, bf16[6,1024,192]{2,1,0:T(8,128)(2,1)}, f32[6,8,128,128]{3,2,1,0:T(8,128)}) custom-call(bf16[1024,768]{1,0:T(8,128)(2,1)} %x_ref.3, bf16[3,768,384]{2,1,0:T(8,128)(2,1)} %w_ref.3, f32[2,384]{1,0:T(2,128)} %bias_ref.1, s32[3,2,1024]{2,1,0:T(2,128)} %copy-done.7, s32[3,1024,2]{2,1,0:T(8,128)} %bitcast.67), custom_call_target="tpu_custom_call" | custom-call | flops 12000000000 | bytes 12000000 | tf_op jit(solution)/shard_map/attend/pallas_call | solution.py:123
  57.9 1.8 collective-permute-start
  59.9 1.1 pad_maximum_fusion
  61.9 1.6 copy.33
  64.3 55.4 %collective-permute-done.1.far_out_ref.far_bias_ref = f32[392,768]{1,0:T(8,128)} collective-permute-done((f32[392,768]{1,0:T(8,128)}, f32[392,768]{1,0:T(8,128)}, u32[]{:S(2)}, u32[]{:S(2)}) %collective-permute-start.1) | collective-permute-done | bytes 1204256 | tf_op jit(solution)/shard_map/ppermute | solution.py:46
  119.7 15.3 %lead.1 = (f32[1024,768]{1,0:T(8,128)}, f32[1024,1]{1,0:T(8,128)}, bf16[1024,768]{1,0:T(8,128)(2,1)}, bf16[1024,1536]{1,0:T(8,128)(2,1)}, bf16[1024,1536]{1,0:T(8,128)(2,1)}, /*index=5*/f32[1024,768]{1,0:T(8,128)}) custom-call(bf16[1024,768]{1,0:T(8,128)(2,1)} %x_ref.3, bf16[1024,384]{1,0:T(8,128)(2,1)} %get-tuple-element.48.ctx_ref, ...), custom_call_target="tpu_custom_call" | custom-call | flops 6000000000 | bytes 20000000 | tf_op jit(solution)/shard_map/lead/pallas_call | solution.py:285
  135.0 29.6 %middle.1 = (bf16[1024,768]{1,0:T(8,128)(2,1)}, bf16[1024,768]{1,0:T(8,128)(2,1)}, bf16[1024,1536]{1,0:T(8,128)(2,1)}, f32[1024,768]{1,0:T(8,128)}, bf16[1024,76...) custom-call(f32[1024,768]{1,0:T(8,128)} %get-tuple-element.50.unit_ref, ...), custom_call_target="tpu_custom_call" | custom-call | flops 15000000512 | bytes 30000000 | tf_op jit(solution)/shard_map/middle/pallas_call | solution.py:356
  164.7 12.1 %feed_grads.1 = (f32[768,1536]{1,0:T(8,128)}, f32[768,1536]{1,0:T(8,128)}) custom-call(bf16[1024,768]{1,0:T(8,128)(2,1)} %get-tuple-element.64.nb_ref, bf16[1024,768]{1,0:T(8,128)(2,1)} %get-tuple-element.65.d_feed_ref, bf16[1024,1536]{1,0:T(8,128)(2,1)} %get-tuple-element.66.act_ref, bf16[1024,1536]{1,0:T(8,128)(2,1)} %get-tuple-element.67.d_hidden_ref), custom_call_target="tpu_custom_call" | custom-call | flops 5000000000 | bytes 20000000 | tf_op jit(solution)/shard_map/feed_grads/pallas_call | solution.py:396
  176.8 2.8 constant_dynamic-slice_fusion.1
  179.6 1.6 copy.43
  181.2 1.6 copy-done.1
  182.8 1.7 dynamic-slice_bitcast_fusion
  184.5 39.5 %attend_back.1 = (f32[1024,768]{1,0:T(8,128)}, f32[4,768,384]{2,1,0:T(8,128)}, f32[2,384]{1,0:T(2,128)}) custom-call(bf16[768,1024]{1,0:T(8,128)(2,1)} %bitcast.69, bf16[1024,768]{1,0:T(8,128)(2,1)} %get-tuple-element.56.da_ref, bf16[384,768]{1,0:T(8,128)(2,1)} %ow_ref.1, bf16[1024,384]{1,0:T(8,128)(2,1)} %get-tuple-element.48.ctx_ref, ...), custom_call_target="tpu_custom_call" | custom-call | flops 20000000000 | bytes 20000000 | tf_op jit(solution)/shard_map/attend_back/pallas_call | solution.py:210
  224.0 0.7 reshape.101
  224.7 1.5 collective-permute-start.3
  226.2 4.2 %constant_dynamic-slice_fusion.3 = (f32[4,2,2,2,1,48,384]{6,5,4,3,2,1,0:T(8,128)}, f32[4,2,2,2,1,48,384]{6,5,4,3,2,1,0:T(8,128)S(1)}) fusion(f32[4,2,2,2,2,48,384]{6,5,4,3,2,1,0:T(8,128)} %bitcast.65, s32[]{:T(128)S(6)} %select_n.54, s32[]{:T(128)S(6)} %select_n.55), kind=kLoop, calls=%fused_computation.38 | loop fusion | bytes 9437192 | tf_op jit(solution)/shard_map/jit(dynamic_index_in_dim)/dynamic_slice | solution.py:72
  230.4 1.7 copy.44
  232.7 3.9 %collective-permute-done.8 = f32[8,1152]{1,0:T(8,128)S(1)} collective-permute-done((f32[8,1152]{1,0:T(8,128)S(1)}, f32[8,1152]{1,0:T(8,128)S(1)}, u32[]{:S(2)}, u32[]{:S(2)}) %collective-permute-start.8) | collective-permute-done | bytes 36896 | tf_op jit(solution)/shard_map/ppermute | solution.py:50
  236.7 1.5 collective-permute-start.9
  238.2 2.4 collective-permute-done.9
  240.6 1.6 collective-permute-start.10
  242.2 2.4 collective-permute-done.10
  244.6 3.5 collective-permute-start.11
  248.1 1.9 collective-permute-done.11
  251.9 2.0 bitcast_add_fusion
  254.1 1.6 collective-permute-start.17
  255.6 2.8 bitcast_add_fusion.1
  258.5 1.6 collective-permute-start.13
  260.2 2.1 bitcast_add_fusion.2
  263.0 32.6 %collective-permute-done.3 = f32[1024,768]{1,0:T(8,128)} collective-permute-done((f32[1024,768]{1,0:T(8,128)}, f32[1024,768]{1,0:T(8,128)}, u32[]{:S(2)}, u32[]{:S(2)}) %collective-permute-start.3) | collective-permute-done | bytes 3145760 | tf_op jit(solution)/shard_map/ppermute | solution.py:46
  295.6 3.7 %add_convert_fusion = bf16[1024,768]{1,0:T(8,128)(2,1)} fusion(f32[1024,768]{1,0:T(8,128)} %collective-permute-done.3, f32[1024,768]{1,0:T(8,128)S(1)} %copy-done.2, f32[1024,768]{1,0:T(8,128)S(1)} %copy-done.3), kind=kLoop, calls=%fused_computation.3 | loop fusion | flops 2359296 | bytes 11010048 | tf_op jit(solution)/shard_map/convert_element_type | solution.py:481
  299.5 1.6 collective-permute-start.18
  301.3 3.6 collective-permute-start.14
  305.3 1.6 collective-permute-start.6
  307.0 21.2 %collective-permute-done.18 = f32[2,48,1536]{2,1,0:T(8,128)S(1)} collective-permute-done((f32[2,48,1536]{2,1,0:T(8,128)S(1)}, f32[2,48,1536]{2,1,0:T(8,128)S(1)}, u32[]{:S(2)}, u32[]{:S(2)}) %collective-permute-start.18) | collective-permute-done | bytes 589856 | tf_op jit(solution)/shard_map/ppermute | solution.py:50
  328.3 1.1 collective-permute-start.19
  329.9 1.7 collective-permute-start.15
  331.6 14.6 %collective-permute-done.6 = f32[4,2,48,384]{3,2,1,0:T(8,128)S(1)} collective-permute-done((f32[4,2,48,384]{3,2,1,0:T(8,128)S(1)}, f32[4,2,48,384]{3,2,1,0:T(8,128)S(1)}, u32[]{:S(2)}, u32[]{:S(2)}) %collective-permute-start.6) | collective-permute-done | bytes 589856 | tf_op jit(solution)/shard_map/ppermute | solution.py:50
  346.3 2.6 collective-permute-start.7
  348.9 0.7 fusion.2
  349.7 12.1 %collective-permute-done.7 = f32[4,48,384]{2,1,0:T(8,128)S(1)} collective-permute-done((f32[4,48,384]{2,1,0:T(8,128)S(1)}, f32[4,48,384]{2,1,0:T(8,128)S(1)}, u32[]{:S(2)}, u32[]{:S(2)}) %collective-permute-start.7) | collective-permute-done | bytes 294944 | tf_op jit(solution)/shard_map/ppermute | solution.py:50
  361.8 0.7 slice.76
  363.1 0.7 bitcast_add_fusion.10
  (99 shorter events, 7.7 us)
Async XLA Ops:
  7.2 127.9 %all-gather.2.cloned.1.call-start = ((), (), s32[]{:S(2)}) async-start(), calls=%async_computation | async-start | bytes 10027008 | tf_op jit(solution)/shard_map/all_gather | solution.py:437
  9.0 17.6 %copy-start.9 = (s32[6,1,1024]{2,1,0:T(1,128)S(1)}, s32[6,1,1024]{2,1,0:T(1,128)}, u32[]{:S(2)}) copy-start(s32[6,1,1024]{2,1,0:T(1,128)} %param.18) | copy-start | bytes 73732
  9.4 16.3 %collective-permute-start.2 = (f32[192,768]{1,0:T(8,128)S(1)}, f32[192,768]{1,0:T(8,128)S(1)}, u32[]{:S(2)}, u32[]{:S(2)}) collective-permute-start(f32[192,768]{1,0:T(8,128)S(1)} %fusion.3), channel_id=1, source_target_pairs={{0,1},{1,0},{2,3},{3,2},{4,5},{5,4},{6,7},{7,6},{8,9},{9,8},{10,11... | collective-permute-start | bytes 1769480 | tf_op jit(solution)/shard_map/ppermute | solution.py:46
  25.7 0.9 copy-start.6
  26.7 1.7 copy-start.7
  28.4 31.3 %copy-start.5 = (bf16[384,768]{1,0:T(8,128)(2,1)S(1)}, bf16[384,768]{1,0:T(8,128)(2,1)}, u32[]{:S(2)}) copy-start(bf16[384,768]{1,0:T(8,128)(2,1)} %ow_ref.1) | copy-start | bytes 1769476
  28.4 31.4 %copy-start.8 = (f32[1536]{0:T(1024)S(1)}, f32[1536]{0:T(1024)}, u32[]{:S(2)}) copy-start(f32[1536]{0:T(1024)} %param.26) | copy-start | bytes 18436
  57.9 4.0 %copy-start.4 = (bf16[1024,768]{1,0:T(8,128)(2,1)S(1)}, bf16[1024,768]{1,0:T(8,128)(2,1)}, u32[]{:S(2)}) copy-start(bf16[1024,768]{1,0:T(8,128)(2,1)} %x_ref.3) | copy-start | bytes 4718596
  57.9 61.8 %collective-permute-start = (f32[1024,384]{1,0:T(8,128)}, f32[1024,384]{1,0:T(8,128)}, u32[]{:S(2)}, u32[]{:S(2)}) collective-permute-start(f32[1024,384]{1,0:T(8,128)} %get-tuple-element.49), channel_id=1, source_target_pairs={{0,1},{1,0},{2,3},{3,2},{4,5},{5,4},{6,7},{7,6},{8,9},{9,8},{10,11... | collective-permute-start | bytes 4718600 | tf_op jit(solution)/shard_map/ppermute | solution.py:46
  59.9 3.7 copy-start.12
  59.9 3.7 copy-start.13
  59.9 3.7 copy-start.14
  59.9 3.7 copy-start.15
  59.9 3.7 %copy-start.16 = (f32[768]{0:T(1024)S(1)}, f32[768]{0:T(1024)}, u32[]{:S(2)}) copy-start(f32[768]{0:T(1024)} %param.29) | copy-start | bytes 9220
  59.9 3.7 %copy-start.17 = (f32[768]{0:T(1024)S(1)}, f32[768]{0:T(1024)}, u32[]{:S(2)}) copy-start(f32[768]{0:T(1024)} %param.30) | copy-start | bytes 9220
  61.1 58.7 %collective-permute-start.1 = (f32[392,768]{1,0:T(8,128)}, f32[392,768]{1,0:T(8,128)}, u32[]{:S(2)}, u32[]{:S(2)}) collective-permute-start(f32[392,768]{1,0:T(8,128)} %pad_maximum_fusion), channel_id=1, source_target_pairs={{0,1},{1,0},{2,3},{3,2},{4,5},{5,4},{6,7},{7,6},{8,9},{9,8},{10,11... | collective-permute-start | bytes 3612680 | tf_op jit(solution)/shard_map/ppermute | solution.py:46
  179.6 3.2 copy-start.1
  181.2 70.7 %collective-permute-start.16 = (f32[2,2,2,48,1536]{4,3,1,0,2:T(8,128)}, f32[2,2,2,48,1536]{4,3,1,0,2:T(8,128)}, u32[]{:S(2)}, u32[]{:S(2)}) collective-permute-start(f32[2,2,2,48,1536]{4,3,1,0,2:T(8,128)} %bitcast.61), channel_id=1, source_target_pairs={{0,2},{2,0},{4,6},{6,4},{8,10},{10,8},{12,14},{14,12},{16,18},{18,... | collective-permute-start | bytes 7077896 | tf_op jit(solution)/shard_map/ppermute | solution.py:50
  184.5 71.1 %collective-permute-start.12 = (f32[2,2,2,48,1536]{4,3,2,1,0:T(8,128)}, f32[2,2,2,48,1536]{4,3,2,1,0:T(8,128)}, u32[]{:S(2)}, u32[]{:S(2)}) collective-permute-start(f32[2,2,2,48,1536]{4,3,2,1,0:T(8,128)} %dynamic-slice_bitcast_fusion), channel_id=1, source_target_pairs={{0,2},{2,0},{4,6},{6,4},{8,10},{10,8},{12,14},{14,12},{16,18},{18,... | collective-permute-start | bytes 7077896 | tf_op jit(solution)/shard_map/ppermute | solution.py:50
  184.5 40.2 %copy-start.10 = (f32[8,768]{1,0:T(8,128)S(1)}, f32[8,768]{1,0:T(8,128)}, u32[]{:S(2)}) copy-start(f32[8,768]{1,0:T(8,128)} %get-tuple-element.61) | copy-start | bytes 73732
  224.7 70.9 %collective-permute-start.3 = (f32[1024,768]{1,0:T(8,128)}, f32[1024,768]{1,0:T(8,128)}, u32[]{:S(2)}, u32[]{:S(2)}) collective-permute-start(f32[1024,768]{1,0:T(8,128)} %get-tuple-element.59), channel_id=1, source_target_pairs={{0,1},{1,0},{2,3},{3,2},{4,5},{5,4},{6,7},{7,6},{8,9},{9,8},{10,11... | collective-permute-start | bytes 9437192 | tf_op jit(solution)/shard_map/ppermute | solution.py:46
  230.4 1.9 copy-start.11
  232.1 28.1 %collective-permute-start.4 = (f32[4,2,2,2,48,384]{5,4,2,1,0,3:T(8,128)}, f32[4,2,2,2,48,384]{5,4,2,1,0,3:T(8,128)}, u32[]{:S(2)}, u32[]{:S(2)}) collective-permute-start(f32[4,2,2,2,48,384]{5,4,2,1,0,3:T(8,128)} %bitcast.62), channel_id=1, source_target_pairs={{0,2},{2,0},{4,6},{6,4},{8,10},{10,8},{12,14},{14,12},{16,18},{18,... | collective-permute-start | bytes 7077896 | tf_op jit(solution)/shard_map/ppermute | solution.py:50
  232.4 4.3 %collective-permute-start.8 = (f32[8,1152]{1,0:T(8,128)S(1)}, f32[8,1152]{1,0:T(8,128)S(1)}, u32[]{:S(2)}, u32[]{:S(2)}) collective-permute-start(f32[8,1152]{1,0:T(8,128)S(1)} %reshape.102), channel_id=1, source_target_pairs={{0,2},{2,0},{4,6},{6,4},{8,10},{10,8},{12,14},{14,12},{16,18},{18,... | collective-permute-start | bytes 110600 | tf_op jit(solution)/shard_map/ppermute | solution.py:50
  236.7 4.0 %collective-permute-start.9 = (f32[8,1152]{1,0:T(8,128)S(1)}, f32[8,1152]{1,0:T(8,128)S(1)}, u32[]{:S(2)}, u32[]{:S(2)}) collective-permute-start(f32[8,1152]{1,0:T(8,128)S(1)} %add.130), channel_id=1, source_target_pairs={{0,4},{2,6},{4,0},{6,2},{8,12},{10,14},{12,8},{14,10},{16,20},{18,... | collective-permute-start | bytes 110600 | tf_op jit(solution)/shard_map/ppermute | solution.py:50
  240.6 4.0 %collective-permute-start.10 = (f32[8,1152]{1,0:T(8,128)S(1)}, f32[8,1152]{1,0:T(8,128)S(1)}, u32[]{:S(2)}, u32[]{:S(2)}) collective-permute-start(f32[8,1152]{1,0:T(8,128)S(1)} %add.131), channel_id=1, source_target_pairs={{0,8},{2,10},{4,12},{6,14},{8,0},{10,2},{12,4},{14,6},{16,24},{18,... | collective-permute-start | bytes 110600 | tf_op jit(solution)/shard_map/ppermute | solution.py:50
  244.6 5.5 %collective-permute-start.11 = (f32[8,1152]{1,0:T(8,128)S(1)}, f32[8,1152]{1,0:T(8,128)S(1)}, u32[]{:S(2)}, u32[]{:S(2)}) collective-permute-start(f32[8,1152]{1,0:T(8,128)S(1)} %add.132), channel_id=1, source_target_pairs={{0,16},{2,18},{4,20},{6,22},{8,24},{10,26},{12,28},{14,30},{16,0},... | collective-permute-start | bytes 110600 | tf_op jit(solution)/shard_map/ppermute | solution.py:50
  254.1 45.3 %collective-permute-start.17 = (f32[2,2,48,1536]{3,2,1,0:T(8,128)S(1)}, f32[2,2,48,1536]{3,2,1,0:T(8,128)S(1)}, u32[]{:S(2)}, u32[]{:S(2)}) collective-permute-start(f32[2,2,48,1536]{3,2,1,0:T(8,128)S(1)} %dynamic-slice_bitcast_fusion.1), channel_id=1, source_target_pairs={{0,4},{2,6},{4,0},{6,2},{8,12},{10,14},{12,8},{14,10},{16,20},{18,... | collective-permute-start | bytes 3538952 | tf_op jit(solution)/shard_map/ppermute | solution.py:50
  258.4 1.8 copy-start
  258.5 42.6 %collective-permute-start.13 = (f32[2,2,48,1536]{3,2,1,0:T(8,128)S(1)}, f32[2,2,48,1536]{3,2,1,0:T(8,128)S(1)}, u32[]{:S(2)}, u32[]{:S(2)}) collective-permute-start(f32[2,2,48,1536]{3,2,1,0:T(8,128)S(1)} %dynamic-slice_bitcast_fusion.2), channel_id=1, source_target_pairs={{0,8},{2,10},{4,12},{6,14},{8,0},{10,2},{12,4},{14,6},{16,24},{18,... | collective-permute-start | bytes 3538952 | tf_op jit(solution)/shard_map/ppermute | solution.py:50
  260.2 35.4 %copy-start.2 = (f32[1024,768]{1,0:T(8,128)S(1)}, f32[1024,768]{1,0:T(8,128)}, u32[]{:S(2)}) copy-start(f32[1024,768]{1,0:T(8,128)} %get-tuple-element.55) | copy-start | bytes 9437188
  260.2 35.4 %copy-start.3 = (f32[1024,768]{1,0:T(8,128)S(1)}, f32[1024,768]{1,0:T(8,128)}, u32[]{:S(2)}) copy-start(f32[1024,768]{1,0:T(8,128)} %get-tuple-element.59) | copy-start | bytes 9437188
  262.4 42.7 %collective-permute-start.5 = (f32[4,2,2,48,384]{4,3,2,1,0:T(8,128)S(1)}, f32[4,2,2,48,384]{4,3,2,1,0:T(8,128)S(1)}, u32[]{:S(2)}, u32[]{:S(2)}) collective-permute-start(f32[4,2,2,48,384]{4,3,2,1,0:T(8,128)S(1)} %dynamic-slice_bitcast_fusion.3), channel_id=1, source_target_pairs={{0,4},{2,6},{4,0},{6,2},{8,12},{10,14},{12,8},{14,10},{16,20},{18,... | collective-permute-start | bytes 3538952 | tf_op jit(solution)/shard_map/ppermute | solution.py:50
  299.5 28.6 %collective-permute-start.18 = (f32[2,48,1536]{2,1,0:T(8,128)S(1)}, f32[2,48,1536]{2,1,0:T(8,128)S(1)}, u32[]{:S(2)}, u32[]{:S(2)}) collective-permute-start(f32[2,48,1536]{2,1,0:T(8,128)S(1)} %dynamic-slice_bitcast_fusion.4), channel_id=1, source_target_pairs={{0,8},{2,10},{4,12},{6,14},{8,0},{10,2},{12,4},{14,6},{16,24},{18,... | collective-permute-start | bytes 1769480 | tf_op jit(solution)/shard_map/ppermute | solution.py:50
  301.3 28.5 %collective-permute-start.14 = (f32[2,48,1536]{2,1,0:T(8,128)S(1)}, f32[2,48,1536]{2,1,0:T(8,128)S(1)}, u32[]{:S(2)}, u32[]{:S(2)}) collective-permute-start(f32[2,48,1536]{2,1,0:T(8,128)S(1)} %dynamic-slice_bitcast_fusion.5), channel_id=1, source_target_pairs={{0,16},{2,18},{4,20},{6,22},{8,24},{10,26},{12,28},{14,30},{16,0},... | collective-permute-start | bytes 1769480 | tf_op jit(solution)/shard_map/ppermute | solution.py:50
  305.3 40.9 %collective-permute-start.6 = (f32[4,2,48,384]{3,2,1,0:T(8,128)S(1)}, f32[4,2,48,384]{3,2,1,0:T(8,128)S(1)}, u32[]{:S(2)}, u32[]{:S(2)}) collective-permute-start(f32[4,2,48,384]{3,2,1,0:T(8,128)S(1)} %dynamic-slice_bitcast_fusion.6), channel_id=1, source_target_pairs={{0,8},{2,10},{4,12},{6,14},{8,0},{10,2},{12,4},{14,6},{16,24},{18,... | collective-permute-start | bytes 1769480 | tf_op jit(solution)/shard_map/ppermute | solution.py:50
  328.3 20.7 %collective-permute-start.19 = (f32[48,1536]{1,0:T(8,128)S(1)}, f32[48,1536]{1,0:T(8,128)S(1)}, u32[]{:S(2)}, u32[]{:S(2)}) collective-permute-start(f32[48,1536]{1,0:T(8,128)S(1)} %dynamic-slice_bitcast_fusion.7), channel_id=1, source_target_pairs={{0,16},{2,18},{4,20},{6,22},{8,24},{10,26},{12,28},{14,30},{16,0},... | collective-permute-start | bytes 884744 | tf_op jit(solution)/shard_map/ppermute | solution.py:50
  329.9 33.2 %collective-permute-start.15 = (f32[48,1536]{1,0:T(8,128)S(1)}, f32[48,1536]{1,0:T(8,128)S(1)}, u32[]{:S(2)}, u32[]{:S(2)}) collective-permute-start(f32[48,1536]{1,0:T(8,128)S(1)} %dynamic-slice_bitcast_fusion.8), channel_id=1, source_target_pairs={{0,4},{2,6},{4,0},{6,2},{8,12},{10,14},{12,8},{14,10},{16,20},{18,... | collective-permute-start | bytes 884744 | tf_op jit(solution)/shard_map/ppermute | solution.py:50
  346.3 15.5 %collective-permute-start.7 = (f32[4,48,384]{2,1,0:T(8,128)S(1)}, f32[4,48,384]{2,1,0:T(8,128)S(1)}, u32[]{:S(2)}, u32[]{:S(2)}) collective-permute-start(f32[4,48,384]{2,1,0:T(8,128)S(1)} %dynamic-slice_bitcast_fusion.9), channel_id=1, source_target_pairs={{0,16},{2,18},{4,20},{6,22},{8,24},{10,26},{12,28},{14,30},{16,0},... | collective-permute-start | bytes 884744 | tf_op jit(solution)/shard_map/ppermute | solution.py:50
Sparse Core Ops, SparseCore 0:
  26.8 83.8 all-gather.1
